TPU v7x, 512 devices: a whole 4x4x16 slice. The times are simulated.
512 devices in a mesh: rep: 8 (over y, z_hi), fsdp: 64 (over x, z_lo, core).
Axes of the slice: x: 4, y: 4, z: 16 (z_hi: 2, z_lo: 8; z = z_hi * 8 + z_lo), core: 2. Of those that a mesh axis runs over, the one named last changes fastest.
Arguments:
- tokens: bfloat16 [131072, 4096], P(('rep', 'fsdp')), may hold values from -24 to 24
- queries: bfloat16 [131072, 2048], P(('rep', 'fsdp')), may hold values from -182 to 182
- key_vectors: bfloat16 [131072, 256], P(('rep', 'fsdp')), may hold values from -5 to 5
- cotangent: bfloat16 [131072, 2048], P(('rep', 'fsdp')), may hold values from -0.1875 to 0.1875
- positions: int32 [131072], P(('rep', 'fsdp')), may hold values from 0 to 4351, as said below
- doc_ids: int32 [131072], P(('rep', 'fsdp')), may hold values from 0 to 254, as said below
- weight: float32 [4096, 256], P('fsdp'), may hold values from -0.09375 to 0.09375
- moment_one: float32 [4096, 256], P('fsdp'), may hold values from -16 to 16
- moment_two: float32 [4096, 256], P('fsdp'), may hold values from 1 to 100
- old_ids: int32 [64], replicated, may hold values from 0 to 63, each once
- new_ids: int32 [64], replicated, may hold values from 0 to 31, as said below
Outputs:
- new_weight: float32 [8192, 256], P('fsdp')
- new_moment_one: float32 [8192, 256], P('fsdp')
- new_moment_two: float32 [8192, 256], P('fsdp')
- token_loss: float32 [131072], P(('rep', 'fsdp'))
Inputs may be any that keep to these rules, and one draw needn't show every extreme that they name: `new_ids`: each new shard number is held by exactly two indices. `doc_ids`: along each sequence of 256 tokens the numbers start at 0 and never fall. Within one document of a sequence, positions rise by one from token to token.
All inputs are finite; a program needn't handle non-finite values.
Results may differ from a plain program's by a relative error of at most 0.008.
Values may be sent and summed in bfloat16 or wider, within the bound.
A program may use at most 64 MiB of HBM per device.

v0:
```python
import math

import jax
import jax.numpy as jnp
from jax import lax
from jax.sharding import PartitionSpec as P

HEADS = 32
KV_HEADS = 4
HEAD_DIM = 64


rope_base = 500000.0
learn_rate = 0.0003 * math.sqrt(2.0)
beta_one = 0.9
beta_two = 0.95
adam_eps = 1e-08
decay_rate = 0.1
step_count = 40


def rotate(values, places):
    half_dim = values.shape[-1] // 2
    frequency = rope_base ** (-(jnp.arange(half_dim, dtype=jnp.float32) * 2.0 / values.shape[-1]))
    angles = places.astype(jnp.float32)[:, None] * frequency[None, :]
    target_shape = (angles.shape[0],) + (1,) * (values.ndim - 2) + (half_dim,)
    cosine = jnp.cos(angles).reshape(target_shape)
    sine_part = jnp.sin(angles).reshape(target_shape)
    first_part = values[..., :half_dim]
    second_part = values[..., half_dim:]
    return jnp.concatenate(
        [
            first_part * cosine - second_part * sine_part,
            second_part * cosine + first_part * sine_part,
        ],
        axis=-1,
    )


def adam_step(weight, moment_one, moment_two, gradient):
    moment_new = beta_one * moment_one + (1.0 - beta_one) * gradient
    second_new = beta_two * moment_two + (1.0 - beta_two) * gradient * gradient
    first_fix = 1.0 - beta_one**step_count
    second_fix = 1.0 - beta_two**step_count
    update = moment_new / first_fix / (jnp.sqrt(second_new / second_fix) + adam_eps)
    weight_new = weight - learn_rate * (update + decay_rate * weight)
    return (weight_new, moment_new, second_new)


def pair_tables(old_ids, new_ids):
    device_count = old_ids.shape[0]
    inverse = (
        jnp.zeros((device_count,), jnp.int32)
        .at[old_ids]
        .set(jnp.arange(device_count, dtype=jnp.int32))
    )
    wanted = 2 * new_ids[None, :] + jnp.arange(2, dtype=jnp.int32)[:, None]
    return inverse[wanted]


def move_state(weight, moment_one, moment_two, sources):
    kv_cols = weight.shape[1]
    spread = (
        lax.all_to_all(weight, "fsdp", split_axis=0, concat_axis=0, tiled=True),
        lax.all_to_all(moment_one, "fsdp", split_axis=0, concat_axis=0, tiled=True),
        lax.all_to_all(moment_two, "fsdp", split_axis=0, concat_axis=0, tiled=True),
    )
    paired = (
        lax.all_to_all(spread[0][sources], "fsdp", split_axis=1, concat_axis=1, tiled=True),
        lax.all_to_all(spread[1][sources], "fsdp", split_axis=1, concat_axis=1, tiled=True),
        lax.all_to_all(spread[2][sources], "fsdp", split_axis=1, concat_axis=1, tiled=True),
    )
    return tuple((moved_rows.reshape(-1, kv_cols) for moved_rows in paired))


def shards(
    tokens,
    queries,
    key_vectors,
    cotangent,
    positions,
    doc_ids,
    weight,
    moment_one,
    moment_two,
    old_ids,
    new_ids,
):
    length = tokens.shape[0]
    shard_rows = weight.shape[0]
    kv_cols = weight.shape[1]
    group_size = HEADS // KV_HEADS
    sources = pair_tables(old_ids, new_ids)
    block_cols = (
        old_ids[:, None] * shard_rows + jnp.arange(shard_rows, dtype=jnp.int32)[None, :]
    ).reshape(-1)
    permuted = jnp.take(tokens, block_cols, axis=1)
    columns = permuted
    value_sum = jnp.dot(
        columns,
        lax.all_gather(weight.astype(jnp.bfloat16), "fsdp", axis=0, tiled=True),
        preferred_element_type=jnp.float32,
    )
    values = value_sum.astype(jnp.bfloat16).reshape(length, KV_HEADS, HEAD_DIM)
    query_rot = rotate(
        queries.astype(jnp.float32).reshape(length, KV_HEADS, group_size, HEAD_DIM), positions
    ).astype(jnp.bfloat16)
    key_rot = rotate(
        key_vectors.astype(jnp.float32).reshape(length, KV_HEADS, HEAD_DIM), positions
    ).astype(jnp.bfloat16)
    scores = jnp.einsum(
        "tkgd,ukd->kgtu", query_rot, key_rot, preferred_element_type=jnp.float32
    ) / math.sqrt(HEAD_DIM)
    token_index = jnp.arange(length, dtype=jnp.int32)
    allowed = (token_index[None, :] <= token_index[:, None]) & (
        doc_ids[None, :] == doc_ids[:, None]
    )
    scores = jnp.where(allowed[None, None], scores, -1e30)
    row_peak = jnp.max(scores, axis=-1, keepdims=True)
    raised = jnp.exp(scores - row_peak)
    attention_probs = raised / jnp.sum(raised, axis=-1, keepdims=True)
    rounded_probs = attention_probs.astype(jnp.bfloat16)
    upstream = cotangent.reshape(length, KV_HEADS, group_size, HEAD_DIM)
    mixed_out = jnp.einsum(
        "kgtu,ukd->tkgd", rounded_probs, values, preferred_element_type=jnp.float32
    )
    token_loss = jnp.sum(mixed_out * upstream.astype(jnp.float32), axis=(1, 2, 3))
    value_grad = jnp.einsum(
        "kgtu,tkgd->ukd", rounded_probs, upstream, preferred_element_type=jnp.float32
    )
    value_grad = value_grad.astype(jnp.bfloat16).reshape(length, kv_cols)
    columns = permuted
    grad_shard = lax.psum_scatter(
        lax.dot_general(
            columns, value_grad, (((0,), (0,)), ((), ())), preferred_element_type=jnp.float32
        ),
        "fsdp",
        scatter_dimension=0,
        tiled=True,
    )
    gradient = lax.psum(grad_shard.astype(jnp.bfloat16), "rep").astype(jnp.float32)
    stepped = adam_step(weight, moment_one, moment_two, gradient)
    outputs = move_state(stepped[0], stepped[1], stepped[2], sources)
    return (outputs[0], outputs[1], outputs[2], token_loss)


def solution(mesh):
    in_specs = (
        P(("rep", "fsdp"), None),
        P(("rep", "fsdp"), None),
        P(("rep", "fsdp"), None),
        P(("rep", "fsdp"), None),
        P(("rep", "fsdp")),
        P(("rep", "fsdp")),
        P("fsdp", None),
        P("fsdp", None),
        P("fsdp", None),
        P(),
        P(),
    )
    out_specs = (P("fsdp", None), P("fsdp", None), P("fsdp", None), P(("rep", "fsdp")))
    return jax.shard_map(shards, mesh=mesh, in_specs=in_specs, out_specs=out_specs, check_vma=False)
```

profile of v0, /device:TPU:1, one launch (start us, length us, event | category | flops | bytes accessed | tf_op | source)
XLA Modules:
  0.0 699.1 jit_solution(10799459660756999198)
XLA Ops:
  12.1 1.5 copy.42
  13.6 3.3 copy.39
  16.9 2.5 fusion.7
  19.4 2.3 fusion.26
  22.8 2.0 copy-done
  26.2 17.0 %gather_fusion = bf16[4096,256]{1,0:T(8,128)(2,1)} fusion(bf16[256,4096]{0,1:T(8,128)(2,1)S(1)} %copy.39, s32[4096]{0:T(1024)S(1)} %broadcast_clamp_fusion), kind=kCustom, calls=%fused_computation | custom fusion | bytes 4210688 | tf_op jit(solution)/shard_map/jit(_take)/gather | solution.py:97
  43.2 4.3 fusion.11
  47.6 439.7 %reduce-scatter.2.cloned.1.call-done = f32[64,256]{1,0:T(8,128)} async-done(((f32[4096,256]{1,0:T(8,128)}), f32[64,256]{1,0:T(8,128)}) %reduce-scatter.2.cloned.1.call-update) | async-done | bytes 65552 | tf_op jit(solution)/shard_map/reduce_scatter | solution.py:133
  488.2 70.5 %psum.7 = bf16[64,256]{1,0:T(8,128)(2,1)S(1)} all-reduce(bf16[64,256]{1,0:T(8,128)(2,1)S(1)} %convert_element_type.36), channel_id=1, replica_groups=mesh['rep'=8,'fsdp'=64] {'rep'}, use_global_device_ids=true, to_apply=%region_3.4 | all-reduce | flops 16384 | bytes 65536 | tf_op jit(solution)/shard_map/psum | solution.py:141
  560.1 15.1 %all-to-all-start.2 = ((f32[64,1,256]{2,1,0:T(1,128)}), f32[64,1,256]{2,1,0:T(1,128)S(1)}, u32[]{:S(2)}, u32[]{:S(2)}) async-start(f32[64,1,256]{2,1,0:T(1,128)} %copy.47), calls=%async_computation.3 | async-start | bytes 131072 | tf_op jit(solution)/shard_map/all_to_all | solution.py:65
  575.9 12.2 %all-to-all-done.2 = f32[64,1,256]{2,1,0:T(1,128)S(1)} async-done(((f32[64,1,256]{2,1,0:T(1,128)}), f32[64,1,256]{2,1,0:T(1,128)S(1)}, u32[]{:S(2)}, u32[]{:S(2)}) %all-to-all-start.2) | async-done | bytes 65568 | tf_op jit(solution)/shard_map/all_to_all | solution.py:65
  588.1 5.2 all-to-all-start.4
  596.2 9.9 %all-to-all-done.4 = f32[64,1,256]{2,1,0:T(1,128)S(1)} async-done(((f32[64,1,256]{2,1,0:T(1,128)}), f32[64,1,256]{2,1,0:T(1,128)S(1)}, u32[]{:S(2)}, u32[]{:S(2)}) %all-to-all-start.4) | async-done | bytes 65568 | tf_op jit(solution)/shard_map/all_to_all | solution.py:66
  606.1 5.2 all-to-all-start
  613.0 11.2 %all-to-all-done = f32[64,1,256]{2,1,0:T(1,128)S(1)} async-done(((f32[64,1,256]{2,1,0:T(1,128)}), f32[64,1,256]{2,1,0:T(1,128)S(1)}, u32[]{:S(2)}, u32[]{:S(2)}) %all-to-all-start) | async-done | bytes 65568 | tf_op jit(solution)/shard_map/all_to_all | solution.py:64
  624.2 5.2 all-to-all-start.3
  630.9 13.0 %all-to-all-done.3 = f32[2,64,256]{2,0,1:T(2,128)S(1)} async-done(((f32[2,64,256]{2,0,1:T(2,128)}), f32[2,64,256]{2,0,1:T(2,128)S(1)}, u32[]{:S(2)}, u32[]{:S(2)}) %all-to-all-start.3) | async-done | bytes 131104 | tf_op jit(solution)/shard_map/all_to_all | solution.py:70
  644.0 6.5 all-to-all-start.5
  651.8 1.7 copy.45
  653.5 11.5 %all-to-all-done.5 = f32[2,64,256]{2,0,1:T(2,128)S(1)} async-done(((f32[2,64,256]{2,0,1:T(2,128)}), f32[2,64,256]{2,0,1:T(2,128)S(1)}, u32[]{:S(2)}, u32[]{:S(2)}) %all-to-all-start.5) | async-done | bytes 131104 | tf_op jit(solution)/shard_map/all_to_all | solution.py:71
  665.0 6.5 all-to-all-start.1
  672.9 13.2 %all-to-all-done.1 = f32[2,64,256]{2,0,1:T(2,128)} async-done(((f32[2,64,256]{2,0,1:T(2,128)}), f32[2,64,256]{2,0,1:T(2,128)}, u32[]{:S(2)}, u32[]{:S(2)}) %all-to-all-start.1) | async-done | bytes 131104 | tf_op jit(solution)/shard_map/all_to_all | solution.py:69
  686.0 1.6 copy.46
  687.6 3.3 convolution_convert_fusion
  (66 shorter events, 20.6 us)
Async XLA Ops:
  7.2 3.1 copy-start.3
  7.2 480.2 %reduce-scatter.2.cloned.1.call-start = ((), (), s32[]{:S(2)}) async-start(), calls=%async_computation.7 | async-start | bytes 4259840 | tf_op jit(solution)/shard_map/reduce_scatter | solution.py:133
  10.3 1.7 copy-start.7
  22.8 2.0 copy-start
  47.6 511.1 %copy-start.4 = (f32[64,256]{1,0:T(8,128)S(1)}, f32[64,256]{1,0:T(8,128)}, u32[]{:S(2)}) copy-start(f32[64,256]{1,0:T(8,128)} %param.19) | copy-start | bytes 196612
  47.6 511.1 %copy-start.5 = (f32[64,256]{1,0:T(8,128)S(1)}, f32[64,256]{1,0:T(8,128)}, u32[]{:S(2)}) copy-start(f32[64,256]{1,0:T(8,128)} %param.17) | copy-start | bytes 196612
  47.6 511.1 %copy-start.6 = (f32[64,256]{1,0:T(8,128)S(1)}, f32[64,256]{1,0:T(8,128)}, u32[]{:S(2)}) copy-start(f32[64,256]{1,0:T(8,128)} %param.18) | copy-start | bytes 196612
  47.6 527.6 %copy-start.8 = (s32[64]{0:T(128)S(1)}, s32[64]{0:T(128)}, u32[]{:S(2)}) copy-start(s32[64]{0:T(128)} %param.21) | copy-start | bytes 772
  47.6 640.0 %all-gather.2.cloned.1.call-start = ((), (), s32[]{:S(2)}) async-start(), calls=%async_computation.8 | async-start | bytes 2129920 | tf_op jit(solution)/shard_map/all_gather | solution.py:101
  560.1 28.0 %all-to-all-start.2 = ((f32[64,1,256]{2,1,0:T(1,128)}), f32[64,1,256]{2,1,0:T(1,128)S(1)}, u32[]{:S(2)}, u32[]{:S(2)}) async-start(f32[64,1,256]{2,1,0:T(1,128)} %copy.47), calls=%async_computation.3 | async-start | bytes 131072 | tf_op jit(solution)/shard_map/all_to_all | solution.py:65
  588.1 18.1 %all-to-all-start.4 = ((f32[64,1,256]{2,1,0:T(1,128)}), f32[64,1,256]{2,1,0:T(1,128)S(1)}, u32[]{:S(2)}, u32[]{:S(2)}) async-start(f32[64,1,256]{2,1,0:T(1,128)} %copy.50), calls=%async_computation.5 | async-start | bytes 131072 | tf_op jit(solution)/shard_map/all_to_all | solution.py:66
  606.1 18.1 %all-to-all-start = ((f32[64,1,256]{2,1,0:T(1,128)}), f32[64,1,256]{2,1,0:T(1,128)S(1)}, u32[]{:S(2)}, u32[]{:S(2)}) async-start(f32[64,1,256]{2,1,0:T(1,128)} %copy.44), calls=%async_computation.1 | async-start | bytes 131072 | tf_op jit(solution)/shard_map/all_to_all | solution.py:64
  624.2 19.8 %all-to-all-start.3 = ((f32[2,64,256]{2,0,1:T(2,128)}), f32[2,64,256]{2,0,1:T(2,128)S(1)}, u32[]{:S(2)}, u32[]{:S(2)}) async-start(f32[2,64,256]{2,0,1:T(2,128)} %copy.48), calls=%async_computation.4 | async-start | bytes 262144 | tf_op jit(solution)/shard_map/all_to_all | solution.py:70
  629.4 58.2 %copy-start.2 = (bf16[4096,256]{1,0:T(8,128)(2,1)S(1)}, bf16[4096,256]{1,0:T(8,128)(2,1)}, u32[]{:S(2)}) copy-start(bf16[4096,256]{1,0:T(8,128)(2,1)} %gather_fusion) | copy-start | bytes 6291460
  644.0 21.0 %all-to-all-start.5 = ((f32[2,64,256]{2,0,1:T(2,128)}), f32[2,64,256]{2,0,1:T(2,128)S(1)}, u32[]{:S(2)}, u32[]{:S(2)}) async-start(f32[2,64,256]{2,0,1:T(2,128)} %copy.51), calls=%async_computation.6 | async-start | bytes 262144 | tf_op jit(solution)/shard_map/all_to_all | solution.py:71
  665.0 21.0 %all-to-all-start.1 = ((f32[2,64,256]{2,0,1:T(2,128)}), f32[2,64,256]{2,0,1:T(2,128)}, u32[]{:S(2)}, u32[]{:S(2)}) async-start(f32[2,64,256]{2,0,1:T(2,128)} %copy.45), calls=%async_computation.2 | async-start | bytes 262144 | tf_op jit(solution)/shard_map/all_to_all | solution.py:69
  687.6 3.3 copy-start.1
Sparse Core Ops, SparseCore 0:
  47.7 439.6 reduce-scatter.1
  559.5 122.5 all-gather.1
where the time goes:
time: 700 us; the launch traced here: 699 us
  waiting for transfers between devices  511 us (73%)
  blocking collectives  70.5 us (10%)
  starting transfers between devices  43.8 us (6%)
  local copies, waits for them, and re-layouts  38.9 us (6%)
  between operations  14.4 us (2%)
  matrix products  12.9 us (2%)
  other arithmetic  8.03 us (1%)
    reduce_scatter x1, waiting for transfers between devices, shards(): lax.psum_scatter(lax.dot_general(columns, value_grad, (((0,), (0,)), ((),...  440 us
    psum x1, blocking collectives, shards(): lax.psum(grad_shard.astype(jnp.bfloat16), 'rep').astype(jnp.float32)  70.5 us
    gather x1, local copies, waits for them, and re-layouts, shards(): permuted = jnp.take(tokens, block_cols, axis=1)  17 us
    all_to_all x1, starting transfers between devices, move_state(): lax.all_to_all(moment_one, 'fsdp', split_axis=0, concat_axis=0, tiled=True)  15.1 us
  transfers between devices with their start and end apart: 8, of which 7 were waited for; matrix products, arithmetic and copies ran while one was open for 2% of the time, Pallas kernels for 0%

commit v1 on v0

v1 whole, which is shorter than its diff:
```python
import functools
import math

import jax
import jax.numpy as jnp
from jax import lax
from jax.experimental import pallas as pl
from jax.experimental.pallas import tpu as pltpu
from jax.sharding import PartitionSpec as P

MESH = pl.DeviceIdType.MESH
BF = jnp.bfloat16
F32 = jnp.float32

rope_base = 500000.0
learn_rate = 0.0003 * math.sqrt(2.0)
beta_one = 0.9
beta_two = 0.95
adam_eps = 1e-08
decay_rate = 0.1
step_count = 40

TOK = 256
NB = 32
GROUP = [(dq, dc) for dq in range(4) for dc in range(2) if (dq, dc) != (0, 0)]
Z_OFFS = [-3, -2, -1, 1, 2, 3, 4]


def adam_step(weight, moment_one, moment_two, gradient):
    moment_new = beta_one * moment_one + (1.0 - beta_one) * gradient
    second_new = beta_two * moment_two + (1.0 - beta_two) * gradient * gradient
    first_fix = 1.0 - beta_one**step_count
    second_fix = 1.0 - beta_two**step_count
    update = moment_new / first_fix / (jnp.sqrt(second_new / second_fix) + adam_eps)
    weight_new = weight - learn_rate * (update + decay_rate * weight)
    return (weight_new, moment_new, second_new)


def portion_scratch():
    return dict(
        part=pltpu.VMEM((8, NB, 16, 128), BF),
        core_in=pltpu.VMEM((4, NB, 16, 128), BF),
        q1_out=pltpu.VMEM((3, NB, 16, 128), BF),
        q1_in=pltpu.VMEM((3, NB, 16, 128), BF),
        q2_sum=pltpu.VMEM((NB, 16, 128), F32),
        q2_out=pltpu.VMEM((NB, 16, 128), BF),
        q2_in=pltpu.VMEM((3, 8, 16, 128), BF),
        za_sum=pltpu.VMEM((8, 16, 128), F32),
        za_out=pltpu.VMEM((8, 16, 128), BF),
        za_in=pltpu.VMEM((3, 2, 16, 128), BF),
        zb_sum=pltpu.VMEM((2, 16, 128), F32),
        zb_out=pltpu.VMEM((2, 16, 128), BF),
        zb_in=pltpu.VMEM((3, 16, 128), BF),
        full=pltpu.VMEM((NB, 16, 128), BF),
        pick=pltpu.VMEM((7, 16, 128), BF),
        mine=pltpu.VMEM((8, 16, 128), BF),
    )


def scratch_plan():
    plan = dict(
        state_out=pltpu.VMEM((8, 16, 128), BF),
        moments_out=pltpu.VMEM((8, 32, 128), BF),
        wall=pltpu.VMEM((8, 8, 8, 16, 128), BF),
        mv=pltpu.VMEM((8, 8, 32, 128), BF),
        mv_pick=pltpu.VMEM((7, 2, 32, 128), BF),
        mv_in=pltpu.VMEM((8, 2, 32, 128), BF),
        wnat=pltpu.VMEM((4096, 256), BF),
        probs=pltpu.VMEM((16, 512, 256), BF),
        keys2=pltpu.VMEM((4, 512, 128), BF),
        vals2=pltpu.VMEM((4, 512, 128), BF),
        bias=pltpu.VMEM((256, 256), F32),
        dacc=pltpu.VMEM((2, 2, 256, 128), F32),
        lacc=pltpu.VMEM((8, 256), F32),
        vacc=pltpu.VMEM((256, 256), F32),
    )
    for name in "ab":
        for key, value in portion_scratch().items():
            plan[name + "_" + key] = value
    plan["send"] = pltpu.SemaphoreType.DMA((128,))
    plan["recv"] = pltpu.SemaphoreType.DMA((128,))
    return plan


PLAN = scratch_plan()


def doubled(pair, odd):
    lane = lax.broadcasted_iota(jnp.int32, pair.shape, 1)
    turned = pltpu.roll(pair, 64, 1)
    low, high = (turned, pair) if odd else (pair, turned)
    top = jnp.where(lane < 64, low, 0.0)
    bottom = jnp.where(lane >= 64, high, 0.0)
    return jnp.concatenate([top, bottom], axis=0)


def kernel(
    inv_ref, new_ref, tok_ref, q_ref, k_ref, cot_ref, trig_ref, doc_ref, w_ref, m_ref, v_ref,
    wo_ref, mo_ref, vo_ref, loss_ref, *scratch
):
    s = dict(zip(PLAN, scratch))
    send, recv = s["send"], s["recv"]
    rep = lax.axis_index("rep")
    fs = lax.axis_index("fsdp")
    y = rep // 2
    x = fs // 16
    zl = (fs // 2) % 8
    core = fs % 2
    z = (rep % 2) * 8 + zl
    a, b = z // 4, z % 4
    me_c = x * 2 + core

    def dev(dx=0, dy=0, dz=0, dc=0):
        nx, ny, nz, nc = (x + dx) % 4, (y + dy) % 4, (z + dz + 16) % 16, (core + dc) % 2
        return (ny * 2 + nz // 8, (nx * 8 + nz % 8) * 2 + nc)

    used = [0]
    pending = []

    def copy(src, dst, where):
        idx = used[0]
        used[0] += 1
        made = pltpu.make_async_remote_copy(
            src_ref=src, dst_ref=dst, send_sem=send.at[idx], recv_sem=recv.at[idx],
            device_id=where, device_id_type=MESH,
        )
        made.start()
        pending.append(made)
        return made

    def arrive(copies):
        for made in copies:
            made.wait_recv()

    barrier = pltpu.get_barrier_semaphore()
    partners = [dict(dx=dq, dc=dc) for dq, dc in GROUP]
    partners += [dict(dy=dq, dc=dc) for dq, dc in GROUP if dq]
    partners += [dict(dz=dz) for dz in (-4, -3, -2, -1, 1, 2, 3, 4, 8)]
    for partner in partners:
        pl.semaphore_signal(barrier, inc=1, device_id=dev(**partner), device_id_type=MESH)

    for c in range(8):
        rows, cols = pl.ds(16 * (c // 2), 16), pl.ds(128 * (c % 2), 128)
        s["state_out"][c] = w_ref[rows, cols].astype(BF)
        s["moments_out"][c, 0:16] = m_ref[rows, cols].astype(BF)
        s["moments_out"][c, 16:32] = v_ref[rows, cols].astype(BF)
    s["wall"][me_c, 3, me_c] = s["state_out"][me_c]
    s["mv"][3, me_c] = s["moments_out"][me_c]
    pl.semaphore_wait(barrier, len(partners))

    first = []
    for dq, dc in GROUP:
        to_c = ((x + dq) % 4) * 2 + (core + dc) % 2
        first.append(copy(s["state_out"].at[to_c], s["wall"].at[to_c, 3, me_c], dev(dx=dq, dc=dc)))
        first.append(copy(s["moments_out"].at[to_c], s["mv"].at[3, me_c], dev(dx=dq, dc=dc)))

    lane128 = lax.broadcasted_iota(jnp.int32, (TOK, 128), 1)
    low_half = (lane128 % 64) < 32

    def rotated(pair):
        swapped = jnp.where(low_half, pltpu.roll(pair, 96, 1), pltpu.roll(pair, 32, 1))
        return pair * trig_ref[:, 0:128] + swapped * trig_ref[:, 128:256]

    for i in range(2):
        turned = rotated(k_ref[:, 128 * i:128 * i + 128].astype(F32))
        for odd in range(2):
            s["keys2"][2 * i + odd] = doubled(turned, odd).astype(BF)
    docs = doc_ref[...].astype(F32)
    columns = jnp.transpose(jnp.broadcast_to(docs, (128, TOK)))
    own_row = lax.broadcasted_iota(jnp.int32, (TOK, 128), 0)
    for half in range(2):
        allowed = (own_row <= lane128 + 128 * half) & (columns == docs[:, 128 * half:128 * half + 128])
        s["bias"][:, 128 * half:128 * half + 128] = jnp.where(allowed, 0.0, -1e30)

    def attention(g):
        def pair_step(i, _):
            q = 4 * g + i
            cols = pl.ds(pl.multiple_of(q * 128, 128), 128)
            rq = rotated(q_ref[:, cols].astype(F32)).astype(BF)
            cot = cot_ref[:, cols]
            for odd in range(2):
                scores = lax.dot_general(
                    s["keys2"][g, 256 * odd:256 * odd + 256, :], rq, (((1,), (1,)), ((), ())),
                    preferred_element_type=F32,
                )
                scores = scores * 0.125 + s["bias"][...]
                raised = jnp.exp(scores - jnp.max(scores, axis=0, keepdims=True))
                probs = (raised * (1.0 / jnp.sum(raised, axis=0, keepdims=True))).astype(BF)
                s["probs"][q, 256 * odd:256 * odd + 256, :] = probs
                s["dacc"][g % 2, odd] += jnp.dot(probs, cot, preferred_element_type=F32)
            return 0

        s["dacc"][g % 2] = jnp.zeros((2, 256, 128), F32)
        lax.fori_loop(0, 4, pair_step, 0)

    def partial(name):
        d = s["dacc"]
        low = d[0, 0] + pltpu.roll(d[0, 1], 64, 1)
        high = pltpu.roll(d[1, 0], 64, 1) + d[1, 1]
        grad = jnp.where(lane128 < 64, low, high)
        turned = jnp.transpose(grad).astype(BF)
        out = s[name + "_part"]

        def block(i, _):
            r = jnp.dot(turned, tok_ref[:, pl.ds(pl.multiple_of(i * 512, 512), 512)], preferred_element_type=F32)
            r = r.astype(BF)
            for k in range(4):
                for p in range(8):
                    out[p, 4 * i + k] = r[16 * p:16 * p + 16, 128 * k:128 * k + 128]
            return 0

        lax.fori_loop(0, 8, block, 0)

    def f(value):
        return value.astype(F32)

    def over(n, step, body):
        def run(i, _):
            body(pl.ds(i * step, step))
            return 0

        lax.fori_loop(0, n // step, run, 0)

    class Portion:
        def __init__(self, name):
            self.name = name
            self.q1, self.q2 = (x, y) if name == "a" else (y, x)

        def buf(self, key):
            return s[self.name + "_" + key]

        def at1(self, r, dc=0):
            return dev(dx=r, dc=dc) if self.name == "a" else dev(dy=r, dc=dc)

        def at2(self, r):
            return dev(dy=r) if self.name == "a" else dev(dx=r)

        def send_core(self):
            self.c0 = [copy(self.buf("part").at[pl.ds(4 * (1 - core), 4)], self.buf("core_in"), dev(dc=1))]

        def send_q1(self):
            arrive(self.c0)
            part, came, out = self.buf("part"), self.buf("core_in"), self.buf("q1_out")
            self.c1 = []
            for r in (2, 1, 3):
                to = (self.q1 + r) % 4

                def add(n):
                    out[r - 1, n] = (f(part[core * 4 + to, n]) + f(came[to, n])).astype(BF)

                over(NB, 4, add)
                self.c1.append(copy(out.at[r - 1], self.buf("q1_in").at[r - 1], self.at1(r)))

        def send_q2(self):
            arrive(self.c1)
            part, came, got = self.buf("part"), self.buf("core_in"), self.buf("q1_in")
            total, out = self.buf("q2_sum"), self.buf("q2_out")

            def add(n):
                t = f(part[core * 4 + self.q1, n]) + f(came[self.q1, n])
                t = t + f(got[0, n]) + f(got[1, n]) + f(got[2, n])
                total[n] = t
                out[n] = t.astype(BF)

            over(NB, 4, add)
            self.c2 = []
            for r in (2, 1, 3):
                to = (self.q2 + r) % 4
                self.c2.append(copy(out.at[pl.ds(8 * to, 8)], self.buf("q2_in").at[r - 1], self.at2(r)))

        def send_za(self):
            arrive(self.c2)
            got, total, out = self.buf("q2_in"), self.buf("za_sum"), self.buf("za_out")
            t = self.buf("q2_sum")[pl.ds(8 * self.q2, 8)]
            t = t + f(got[0]) + f(got[1]) + f(got[2])
            total[...] = t
            out[...] = t.astype(BF)
            self.c3 = []
            for r in (2, 1, 3):
                to = (b + r) % 4
                self.c3.append(copy(out.at[pl.ds(2 * to, 2)], self.buf("za_in").at[r - 1], dev(dz=to - b)))

        def send_zb(self):
            arrive(self.c3)
            got, total, out = self.buf("za_in"), self.buf("zb_sum"), self.buf("zb_out")
            t = self.buf("za_sum")[pl.ds(2 * b, 2)] + f(got[0]) + f(got[1]) + f(got[2])
            total[...] = t
            out[...] = t.astype(BF)
            self.c4 = []
            for r in (2, 1, 3):
                self.c4.append(copy(out.at[(a + r) % 2], self.buf("zb_in").at[r - 1], dev(dz=4 * r)))

        def gather_z(self):
            arrive(self.c4)
            got, full = self.buf("zb_in"), self.buf("full")
            slot = 8 * self.q2 + 2 * b + a % 2
            t = self.buf("zb_sum")[a % 2] + f(got[0]) + f(got[1]) + f(got[2])
            full[slot] = t.astype(BF)
            self.c5 = [copy(full.at[slot], full.at[slot], dev(dz=o)) for o in Z_OFFS]

        def gather_q2(self):
            arrive(self.c5)
            full = self.buf("full")
            own = pl.ds(8 * self.q2, 8)
            self.c6 = [copy(full.at[own], full.at[own], self.at2(r)) for r in (2, 1, 3)]

        def exchange(self):
            arrive(self.c6)
            full, pick, mine = self.buf("full"), self.buf("pick"), self.buf("mine")
            piece = core * 4 + self.q1
            self.c7 = []
            for idx, (dq, dc) in enumerate(GROUP):
                to_x = (x + dq) % 4 if self.name == "a" else x
                pick[idx] = full[new_ref[(to_x * 8 + zl) * 2 + (core + dc) % 2]]
                self.c7.append(copy(pick.at[idx], mine.at[piece], self.at1(dq, dc)))
            mine[piece] = full[new_ref[fs]]

        def gradient(self):
            arrive(self.c7)
            return jnp.transpose(f(self.buf("mine")[...]).reshape(128, 128))

    pa, pb = Portion("a"), Portion("b")
    wall, mv = s["wall"], s["mv"]

    def z_step(step):
        out = []
        up, down = 3 + (step - 1), 3 - (step - 1)
        if step < 4:
            pairs = [(up, up + 1, -1, pl.ds(0, 8)), (down, down - 1, 1, pl.ds(0, 8))]
        else:
            pairs = [(6, 7, -1, pl.ds(0, 4)), (0, 7, 1, pl.ds(4, 4))]
        for src, dst, dz, part in pairs:
            out.append(copy(wall.at[me_c, src, part], wall.at[me_c, dst, part], dev(dz=dz)))
            out.append(copy(mv.at[src, part], mv.at[dst, part], dev(dz=dz)))
        return out

    def where(j):
        return ((j // 2) % 8 - zl + 11) % 8, (j // 16) * 2 + j % 2

    attention(0)
    arrive(first)
    ring = z_step(1)
    attention(1)
    partial("a")
    pa.send_core()
    arrive(ring)
    ring = z_step(2)
    attention(2)
    pa.send_q1()
    arrive(ring)
    ring = z_step(3)
    attention(3)
    partial("b")
    pb.send_core()
    arrive(ring)
    ring = z_step(4)
    pa.send_q2()
    pb.send_q1()
    pa.send_za()
    arrive(ring)

    moved = []
    for idx, (dq, dc) in enumerate(GROUP):
        n = new_ref[(((x + dq) % 4) * 8 + zl) * 2 + (core + dc) % 2]
        for i in range(2):
            slot, c = where(inv_ref[2 * n + i])
            s["mv_pick"][idx, i] = mv[slot, c]
        moved.append(copy(s["mv_pick"].at[idx], s["mv_in"].at[me_c], dev(dx=dq, dc=dc)))
    own_n = new_ref[fs]
    for i in range(2):
        slot, c = where(inv_ref[2 * own_n + i])
        s["mv_in"][me_c, i] = mv[slot, c]
    def wcopy(c, part, where_to):
        return copy(wall.at[c, part], wall.at[c, part], where_to)

    all_z = pl.ds(0, 8)
    left_c, right_c = ((x + 3) % 4) * 2 + core, ((x + 1) % 4) * 2 + core
    far_c = ((x + 2) % 4) * 2 + core
    along_x = [wcopy(me_c, all_z, dev(dx=1)), wcopy(me_c, all_z, dev(dx=3))]
    across = [wcopy(me_c, all_z, dev(dc=1))]
    pa.send_zb()
    pb.send_q2()
    pa.gather_z()
    pb.send_za()
    arrive(along_x)
    far = [wcopy(left_c, pl.ds(0, 4), dev(dx=1)), wcopy(right_c, pl.ds(4, 4), dev(dx=3))]
    across += [wcopy(left_c, all_z, dev(dc=1)), wcopy(right_c, all_z, dev(dc=1))]
    pa.gather_q2()
    pb.send_zb()
    pa.exchange()
    pb.gather_z()
    arrive(far)
    across.append(wcopy(far_c, all_z, dev(dc=1)))
    pb.gather_q2()
    arrive(across)

    wnat = s["wnat"]

    def natural(i, _):
        slot, c = where(inv_ref[i])
        base = pl.multiple_of(i * 64, 64)
        for piece in range(8):
            wnat[pl.ds(base + 16 * (piece // 2), 16), 128 * (piece % 2):128 * (piece % 2) + 128] = wall[piece, slot, c]
        return 0

    lax.fori_loop(0, 64, natural, 0)
    pb.exchange()
    s["vacc"][...] = jnp.zeros((256, 256), F32)

    def project(i, _):
        k = pl.ds(pl.multiple_of(i * 512, 512), 512)
        s["vacc"][...] += jnp.dot(tok_ref[:, k], wnat[k, :], preferred_element_type=F32)
        return 0

    lax.fori_loop(0, 8, project, 0)
    for i in range(2):
        pair = s["vacc"][:, 128 * i:128 * i + 128]
        for odd in range(2):
            s["vals2"][2 * i + odd] = doubled(pair, odd).astype(BF)
    s["lacc"][...] = jnp.zeros((8, 256), F32)

    def loss_step(q, _):
        cot = cot_ref[:, pl.ds(pl.multiple_of(q * 128, 128), 128)]
        g = q // 4
        t = lax.dot_general(s["vals2"][g], cot, (((1,), (1,)), ((), ())), preferred_element_type=F32)
        t = t * f(s["probs"][q])
        s["lacc"][...] += jnp.sum(t.reshape(64, 8, 256), axis=0)
        return 0

    lax.fori_loop(0, 16, loss_step, 0)
    loss_ref[...] = jnp.sum(s["lacc"][...], axis=0, keepdims=True)

    arrive(moved)
    grads = [pa.gradient(), pb.gradient()]
    for i in range(2):
        slot, src = where(inv_ref[2 * own_n + i])
        for c in range(8):
            r0, l0 = 64 * i + 16 * (c // 2), 128 * (c % 2)
            weight = f(wall[c, slot, src])
            one = f(s["mv_in"][c, i, 0:16])
            two = f(s["mv_in"][c, i, 16:32])
            new = adam_step(weight, one, two, grads[c % 2][r0:r0 + 16])
            for ref, value in zip((wo_ref, mo_ref, vo_ref), new):
                ref[r0:r0 + 16, l0:l0 + 128] = value
    for made in pending:
        made.wait_send()


def shards(
    tokens, queries, key_vectors, cotangent, positions, doc_ids, weight, moment_one, moment_two, old_ids, new_ids
):
    index = jnp.arange(64, dtype=jnp.int32)
    inverse = jnp.sum(jnp.where(old_ids[None, :] == index[:, None], index[None, :], 0), axis=1)
    lane = jnp.arange(256, dtype=jnp.int32)
    half = (lane % 32).astype(F32)
    frequency = rope_base ** (-(half * 2.0 / 64))
    angles = positions.astype(F32)[:, None] * frequency[None, :]
    signed = jnp.where((lane % 64) < 32, -jnp.sin(angles), jnp.sin(angles))
    trig = jnp.where(lane < 128, jnp.cos(angles), signed)

    vmem = pl.BlockSpec(memory_space=pltpu.VMEM)
    smem = pl.BlockSpec(memory_space=pltpu.SMEM)
    outs = pl.pallas_call(
        kernel,
        out_shape=[jax.ShapeDtypeStruct((128, 256), F32)] * 3 + [jax.ShapeDtypeStruct((1, 256), F32)],
        in_specs=[smem, smem] + [vmem] * 9,
        out_specs=[vmem] * 4,
        scratch_shapes=list(PLAN.values()),
        compiler_params=pltpu.CompilerParams(
            collective_id=0, has_side_effects=True, vmem_limit_bytes=48 * 1024 * 1024
        ),
        cost_estimate=pl.CostEstimate(flops=2_200_000_000, bytes_accessed=6_000_000, transcendentals=2_200_000),
    )(
        inverse, new_ids, tokens, queries, key_vectors, cotangent, trig, doc_ids.reshape(1, 256),
        weight, moment_one, moment_two,
    )
    return (outs[0], outs[1], outs[2], outs[3].reshape(256))


def solution(mesh):
    in_specs = (
        P(("rep", "fsdp"), None),
        P(("rep", "fsdp"), None),
        P(("rep", "fsdp"), None),
        P(("rep", "fsdp"), None),
        P(("rep", "fsdp")),
        P(("rep", "fsdp")),
        P("fsdp", None),
        P("fsdp", None),
        P("fsdp", None),
        P(),
        P(),
    )
    out_specs = (P("fsdp", None), P("fsdp", None), P("fsdp", None), P(("rep", "fsdp")))
    return jax.shard_map(shards, mesh=mesh, in_specs=in_specs, out_specs=out_specs, check_vma=False)
```

time: 700 us -> 98.5 us (0.14)
  the two profiles are of different devices: /device:TPU:1 before, /device:TPU:32 now
where the time goes in v1:
time: 98.5 us; the launch traced here: 98.1 us
  Pallas kernels  83.6 us (85%)
  local copies, waits for them, and re-layouts  11.3 us (11%)
  other arithmetic  2.49 us (3%)
    pallas_call x1, Pallas kernels, shards(): pl.pallas_call(kernel, out_shape=[jax.ShapeDtypeStruct((128, 256), F32)]...  83.6 us
    unnamed x22, local copies, waits for them, and re-layouts  11.3 us

profile of v1, /device:TPU:32, one launch (start us, length us, event | category | flops | bytes accessed | tf_op | source)
XLA Modules:
  0.0 98.1 jit_solution(2913313046278523692)
XLA Ops:
  0.6 0.8 select_reduce_fusion.inv_ref
  1.4 0.7 convert_element_type.10
  2.1 1.0 %fusion.trig_ref = f32[256,256]{1,0:T(8,128)S(1)} fusion(f32[256]{0:T(256)S(1)} %fusion.4, f32[256]{0:T(256)S(1)} %convert_element_type.10, pred[256]{0:T(512)(128)(4,1)S(1)} %get-tuple-element.12, pred[256]{0:T(512)(128)(4,1)S(1)} %get-tuple-element.13), kind=kLoop, calls=%fused_computation.3 | loop fusion | flops 262144 | bytes 264704 | tf_op jit(solution)/shard_map/jit(_where)/select_n | solution.py:459
  3.1 0.0 copy-start
  3.1 1.6 %copy-done = bf16[256,4096]{1,0:T(8,128)(2,1)S(1)} copy-done((bf16[256,4096]{1,0:T(8,128)(2,1)S(1)}, bf16[256,4096]{1,0:T(8,128)(2,1)}, u32[]{:S(2)}) %copy-start) | copy-done | bytes 2097176
  4.7 0.0 copy-start.1
  4.7 1.2 %copy-done.1 = bf16[256,2048]{1,0:T(8,128)(2,1)S(1)} copy-done((bf16[256,2048]{1,0:T(8,128)(2,1)S(1)}, bf16[256,2048]{1,0:T(8,128)(2,1)}, u32[]{:S(2)}) %copy-start.1) | copy-done | bytes 1048600
  5.9 0.0 copy-start.2
  5.9 1.2 %copy-done.2 = bf16[256,2048]{1,0:T(8,128)(2,1)S(1)} copy-done((bf16[256,2048]{1,0:T(8,128)(2,1)S(1)}, bf16[256,2048]{1,0:T(8,128)(2,1)}, u32[]{:S(2)}) %copy-start.2) | copy-done | bytes 1048600
  7.2 0.0 copy-start.3
  7.2 0.9 copy-done.3
  8.1 0.0 copy-start.4
  8.1 0.8 copy-done.4
  8.9 0.0 copy-start.5
  8.9 0.8 copy-done.5
  9.8 0.0 copy-start.6
  9.8 0.8 copy-done.6
  10.6 0.7 copy-done.7
  11.3 0.7 copy-done.8
  11.9 83.6 %shard_map.138 = (f32[128,256]{1,0:T(8,128)S(1)}, f32[128,256]{1,0:T(8,128)S(1)}, f32[128,256]{1,0:T(8,128)S(1)}, f32[1,256]{1,0:T(1,128)S(1)}) custom-call(s32[64]{0:T(128)S(1)} %select_reduce_fusion.inv_ref, s32[64]{0:T(128)S(1)} %copy-done.8, bf16[256,4096]{1,0:T(8,128)(2,1)S(1)} %copy-done, bf16[256,2048]{1,0:T(8,128)(2,1)S(1)} %copy-done.1, ...), custom_call_target="tpu_custom_call" | custom-call | flops 2200000000 | bytes 6000000 | tf_op jit(solution)/shard_map/pallas_call | solution.py:463
  95.5 0.7 copy.19
  96.2 0.7 copy.20
  96.8 0.7 copy.21
  97.5 0.6 copy.22
  (4 shorter events, 0.0 us)
Async XLA Ops:
  3.1 1.6 %copy-start = (bf16[256,4096]{1,0:T(8,128)(2,1)S(1)}, bf16[256,4096]{1,0:T(8,128)(2,1)}, u32[]{:S(2)}) copy-start(bf16[256,4096]{1,0:T(8,128)(2,1)} %tok_ref.1) | copy-start | bytes 6291460
  4.7 1.2 %copy-start.1 = (bf16[256,2048]{1,0:T(8,128)(2,1)S(1)}, bf16[256,2048]{1,0:T(8,128)(2,1)}, u32[]{:S(2)}) copy-start(bf16[256,2048]{1,0:T(8,128)(2,1)} %q_ref.1) | copy-start | bytes 3145732
  5.9 1.2 %copy-start.2 = (bf16[256,2048]{1,0:T(8,128)(2,1)S(1)}, bf16[256,2048]{1,0:T(8,128)(2,1)}, u32[]{:S(2)}) copy-start(bf16[256,2048]{1,0:T(8,128)(2,1)} %cot_ref.1) | copy-start | bytes 3145732
  7.2 0.9 copy-start.3
  8.1 0.8 copy-start.4
  8.9 0.8 copy-start.5
  9.8 0.8 copy-start.6
  10.6 0.7 copy-start.7
  11.3 0.7 copy-start.8

commit v2 on v1

v2 whole, which is shorter than its diff:
```python
import math

import jax
import jax.numpy as jnp
from jax import lax
from jax.experimental import pallas as pl
from jax.experimental.pallas import tpu as pltpu
from jax.sharding import PartitionSpec as P

MESH = pl.DeviceIdType.MESH
BF = jnp.bfloat16
F32 = jnp.float32

rope_base = 500000.0
learn_rate = 0.0003 * math.sqrt(2.0)
beta_one = 0.9
beta_two = 0.95
adam_eps = 1e-08
decay_rate = 0.1
step_count = 40

TOK = 256
NB = 32
GROUP = [(dq, dc) for dq in range(4) for dc in range(2) if (dq, dc) != (0, 0)]


def adam_step(weight, moment_one, moment_two, gradient):
    moment_new = beta_one * moment_one + (1.0 - beta_one) * gradient
    second_new = beta_two * moment_two + (1.0 - beta_two) * gradient * gradient
    first_fix = 1.0 - beta_one**step_count
    second_fix = 1.0 - beta_two**step_count
    update = moment_new / first_fix / (jnp.sqrt(second_new / second_fix) + adam_eps)
    weight_new = weight - learn_rate * (update + decay_rate * weight)
    return (weight_new, moment_new, second_new)


def portion_scratch():
    return dict(
        part=pltpu.VMEM((8, NB, 16, 128), BF),
        core_in=pltpu.VMEM((4, NB, 16, 128), BF),
        q1_out=pltpu.VMEM((3, NB, 16, 128), BF),
        q1_in=pltpu.VMEM((3, NB, 16, 128), BF),
        q2_sum=pltpu.VMEM((NB, 16, 128), F32),
        q2_out=pltpu.VMEM((NB, 16, 128), BF),
        q2_in=pltpu.VMEM((3, 8, 16, 128), BF),
        full=pltpu.VMEM((NB, 16, 128), BF),
        pick=pltpu.VMEM((7, 16, 128), BF),
        mine=pltpu.VMEM((8, 16, 128), BF),
    )


def scratch_plan():
    plan = dict(
        state_out=pltpu.VMEM((8, 32, 128), BF),
        state=pltpu.VMEM((8, 8, 32, 128), BF),
        wall=pltpu.VMEM((8, 8, 8, 16, 128), BF),
        mv_pick=pltpu.VMEM((7, 2, 32, 128), BF),
        mv_in=pltpu.VMEM((8, 2, 32, 128), BF),
        wnat=pltpu.VMEM((4096, 256), BF),
        probs=pltpu.VMEM((16, 512, 256), BF),
        keys2=pltpu.VMEM((4, 512, 128), BF),
        vals2=pltpu.VMEM((4, 512, 128), BF),
        bias=pltpu.VMEM((256, 256), F32),
        dacc=pltpu.VMEM((2, 2, 256, 128), F32),
        lacc=pltpu.VMEM((8, 256), F32),
        vacc=pltpu.VMEM((256, 256), F32),
        z_sum=pltpu.VMEM((2, 8, 16, 128), F32),
        z_out=pltpu.VMEM((2, 8, 16, 128), BF),
        z_in=pltpu.VMEM((15, 2, 16, 128), BF),
        z_all=pltpu.VMEM((2, 8, 16, 128), BF),
        tok=pltpu.VMEM((TOK, 4096), BF),
        q=pltpu.VMEM((TOK, 2048), BF),
        k=pltpu.VMEM((TOK, 256), BF),
        cot=pltpu.VMEM((TOK, 2048), BF),
        doc=pltpu.VMEM((1, TOK), jnp.int32),
        w=pltpu.VMEM((64, 256), F32),
        m=pltpu.VMEM((64, 256), F32),
        v=pltpu.VMEM((64, 256), F32),
    )
    for name in "ab":
        for key, value in portion_scratch().items():
            plan[name + "_" + key] = value
    plan["send"] = pltpu.SemaphoreType.DMA((112,))
    plan["recv"] = pltpu.SemaphoreType.DMA((112,))
    plan["local"] = pltpu.SemaphoreType.DMA((8,))
    return plan


PLAN = scratch_plan()


def doubled(pair, odd):
    lane = lax.broadcasted_iota(jnp.int32, pair.shape, 1)
    turned = pltpu.roll(pair, 64, 1)
    low, high = (turned, pair) if odd else (pair, turned)
    top = jnp.where(lane < 64, low, 0.0)
    bottom = jnp.where(lane >= 64, high, 0.0)
    return jnp.concatenate([top, bottom], axis=0)


def kernel(
    table_ref, trig_ref, w_hbm, m_hbm, v_hbm, k_hbm, doc_hbm, q_hbm, cot_hbm, tok_hbm,
    wo_ref, mo_ref, vo_ref, loss_ref, *scratch
):
    s = dict(zip(PLAN, scratch))
    send, recv = s["send"], s["recv"]
    w_ref, m_ref, v_ref, k_ref, doc_ref, q_ref, cot_ref, tok_ref = (
        s[name] for name in ("w", "m", "v", "k", "doc", "q", "cot", "tok")
    )
    fetches = {}
    for idx, (name, src) in enumerate(
        zip(("w", "m", "v", "k", "doc", "q", "cot", "tok"), (w_hbm, m_hbm, v_hbm, k_hbm, doc_hbm, q_hbm, cot_hbm, tok_hbm))
    ):
        fetches[name] = pltpu.make_async_copy(src, s[name], s["local"].at[idx])
        fetches[name].start()
    rep = lax.axis_index("rep")
    fs = lax.axis_index("fsdp")
    y = lax.div(rep, 2)
    x = lax.div(fs, 16)
    zl = lax.rem(lax.div(fs, 2), 8)
    core = lax.rem(fs, 2)
    z = lax.rem(rep, 2) * 8 + zl
    xs = [x] + [lax.rem(x + d, 4) for d in (1, 2, 3)]
    ys = [y] + [lax.rem(y + d, 4) for d in (1, 2, 3)]
    cores = [core, 1 - core]
    me_c = x * 2 + core

    def dev(dx=0, dy=0, dz=0, dc=0):
        if dz == 0:
            return (ys[dy] * 2 + lax.rem(rep, 2), xs[dx] * 16 + zl * 2 + cores[dc])
        nz = lax.rem(z + (dz + 16), 16)
        return (ys[dy] * 2 + lax.div(nz, 8), xs[dx] * 16 + lax.rem(nz, 8) * 2 + cores[dc])

    def new_of(dx, dc):
        return table_ref[64 + xs[dx] * 16 + zl * 2 + cores[dc]]

    used = [0]
    pending = []

    def copy(src, dst, where):
        idx = used[0]
        used[0] += 1
        made = pltpu.make_async_remote_copy(
            src_ref=src, dst_ref=dst, send_sem=send.at[idx], recv_sem=recv.at[idx],
            device_id=where, device_id_type=MESH,
        )
        made.start()
        pending.append(made)
        return made

    def arrive(copies):
        for made in copies:
            made.wait_recv()

    barrier = pltpu.get_barrier_semaphore()
    partners = [dict(dx=dq, dc=dc) for dq, dc in GROUP]
    partners += [dict(dy=dq, dc=dc) for dq, dc in GROUP if dq]
    partners += [dict(dz=dz) for dz in range(1, 16)]
    for partner in partners:
        pl.semaphore_signal(barrier, inc=1, device_id=dev(**partner), device_id_type=MESH)

    lane128 = lax.broadcasted_iota(jnp.int32, (TOK, 128), 1)
    low_half = (lane128 % 64) < 32

    def rotated(pair):
        swapped = jnp.where(low_half, pltpu.roll(pair, 96, 1), pltpu.roll(pair, 32, 1))
        return pair * trig_ref[:, 0:128] + swapped * trig_ref[:, 128:256]

    for name in ("w", "m", "v"):
        fetches[name].wait()
    for c in range(8):
        rows, cols = pl.ds(16 * (c // 2), 16), pl.ds(128 * (c % 2), 128)
        s["wall"][me_c, 3, c] = w_ref[rows, cols].astype(BF)
        for part, ref in enumerate((m_ref, v_ref)):
            s["state_out"][c, 16 * part:16 * part + 16] = ref[rows, cols].astype(BF)
    s["state"][3, me_c] = s["state_out"][me_c]

    fetches["k"].wait()
    for i in range(2):
        turned = rotated(k_ref[:, 128 * i:128 * i + 128].astype(F32))
        for odd in range(2):
            s["keys2"][2 * i + odd] = doubled(turned, odd).astype(BF)
    fetches["doc"].wait()
    docs = doc_ref[...].astype(F32)
    columns = jnp.transpose(jnp.broadcast_to(docs, (128, TOK)))
    own_row = lax.broadcasted_iota(jnp.int32, (TOK, 128), 0)
    for half in range(2):
        allowed = (own_row <= lane128 + 128 * half) & (columns == docs[:, 128 * half:128 * half + 128])
        s["bias"][:, 128 * half:128 * half + 128] = jnp.where(allowed, 0.0, -1e30)

    pl.semaphore_wait(barrier, len(partners))
    wall = s["wall"]
    own_w = wall.at[me_c, 3]
    along_z = [copy(own_w, wall.at[me_c, 3 - o], dev(dz=o)) for o in (-4, 3, -3, 2, -2, 1, -1)]
    first = []
    for dq, dc in GROUP:
        to_c = xs[dq] * 2 + cores[dc]
        first.append(copy(s["state_out"].at[to_c], s["state"].at[3, me_c], dev(dx=dq, dc=dc)))
    fetches["q"].wait()
    fetches["cot"].wait()
    factor = 0.125 * math.log2(math.e)

    def softmax(keys, queries, bias):
        scores = lax.dot_general(keys, queries, (((1,), (1,)), ((), ())), preferred_element_type=F32)
        scores = scores * factor + bias
        raised = jnp.exp2(scores - jnp.max(scores, axis=0, keepdims=True))
        return (raised * (1.0 / jnp.sum(raised, axis=0, keepdims=True))).astype(BF)

    def attention(g):
        def pair_step(i, _):
            q = 4 * g + i
            cols = pl.ds(pl.multiple_of(q * 128, 128), 128)
            rq = rotated(q_ref[:, cols].astype(F32)).astype(BF)
            cot = cot_ref[:, cols]
            for odd in range(2):
                early = softmax(s["keys2"][g, 256 * odd:256 * odd + 128, :], rq[0:128], s["bias"][0:128, 0:128])
                late = softmax(s["keys2"][g, 256 * odd:256 * odd + 256, :], rq[128:256], s["bias"][:, 128:256])
                early = jnp.concatenate([early, jnp.zeros((128, 128), BF)], axis=0)
                probs = jnp.concatenate([early, late], axis=1)
                s["probs"][q, 256 * odd:256 * odd + 256, :] = probs
                s["dacc"][g % 2, odd] += jnp.dot(probs, cot, preferred_element_type=F32)
            return 0

        s["dacc"][g % 2] = jnp.zeros((2, 256, 128), F32)
        lax.fori_loop(0, 4, pair_step, 0, unroll=2)

    def partial(name):
        d = s["dacc"]
        low = d[0, 0] + pltpu.roll(d[0, 1], 64, 1)
        high = pltpu.roll(d[1, 0], 64, 1) + d[1, 1]
        grad = jnp.where(lane128 < 64, low, high)
        turned = jnp.transpose(grad).astype(BF)
        out = s[name + "_part"]

        def block(i, _):
            r = jnp.dot(turned, tok_ref[:, pl.ds(pl.multiple_of(i * 512, 512), 512)], preferred_element_type=F32)
            r = r.astype(BF)
            for k in range(4):
                for p in range(8):
                    out[p, 4 * i + k] = r[16 * p:16 * p + 16, 128 * k:128 * k + 128]
            return 0

        lax.fori_loop(0, 8, block, 0)

    def f(value):
        return value.astype(F32)

    def over(n, step, body):
        def run(i, _):
            body(pl.ds(i * step, step))
            return 0

        lax.fori_loop(0, n // step, run, 0)

    class Portion:
        def __init__(self, name):
            self.name = name
            self.q1, self.q2 = (x, y) if name == "a" else (y, x)
            self.q1s, self.q2s = (xs, ys) if name == "a" else (ys, xs)
            self.side = 0 if name == "a" else 1

        def buf(self, key):
            return s[self.name + "_" + key]

        def at1(self, r, dc=0):
            return dev(dx=r, dc=dc) if self.name == "a" else dev(dy=r, dc=dc)

        def at2(self, r):
            return dev(dy=r) if self.name == "a" else dev(dx=r)

        def send_core(self):
            self.c0 = [copy(self.buf("part").at[pl.ds(4 * (1 - core), 4)], self.buf("core_in"), dev(dc=1))]

        def send_q1(self):
            arrive(self.c0)
            part, came, out = self.buf("part"), self.buf("core_in"), self.buf("q1_out")
            self.c1 = []
            for r in (2, 1, 3):
                to = self.q1s[r]

                def add(n):
                    out[r - 1, n] = (f(part[core * 4 + to, n]) + f(came[to, n])).astype(BF)

                over(NB, 4, add)
                self.c1.append(copy(out.at[r - 1], self.buf("q1_in").at[r - 1], self.at1(r)))

        def send_q2(self):
            arrive(self.c1)
            part, came, got = self.buf("part"), self.buf("core_in"), self.buf("q1_in")
            total, out = self.buf("q2_sum"), self.buf("q2_out")

            def add(n):
                t = f(part[core * 4 + self.q1, n]) + f(came[self.q1, n])
                t = t + f(got[0, n]) + f(got[1, n]) + f(got[2, n])
                total[n] = t
                out[n] = t.astype(BF)

            over(NB, 4, add)
            self.c2 = []
            for r in (2, 1, 3):
                to = self.q2s[r]
                self.c2.append(copy(out.at[pl.ds(8 * to, 8)], self.buf("q2_in").at[r - 1], self.at2(r)))

        def sum_q2(self):
            arrive(self.c2)
            got, side = self.buf("q2_in"), self.side
            t = self.buf("q2_sum")[pl.ds(8 * self.q2, 8)]
            t = t + f(got[0]) + f(got[1]) + f(got[2])
            s["z_sum"][side] = t
            s["z_out"][side] = t.astype(BF)

        def gather_q2(self):
            full, mine = self.buf("full"), s["z_all"].at[self.side]
            own = pl.ds(8 * self.q2, 8)
            self.c6 = [copy(mine, full.at[own], self.at2(r)) for r in (2, 1, 3)]
            full[own] = mine[...]

        def exchange(self):
            arrive(self.c6)
            full, pick, mine = self.buf("full"), self.buf("pick"), self.buf("mine")
            piece = core * 4 + self.q1
            self.c7 = []
            for idx, (dq, dc) in enumerate(GROUP):
                pick[idx] = full[new_of(dq if self.name == "a" else 0, dc)]
                self.c7.append(copy(pick.at[idx], mine.at[piece], self.at1(dq, dc)))
            mine[piece] = full[new_of(0, 0)]

        def gradient(self):
            arrive(self.c7)
            return jnp.transpose(f(self.buf("mine")[...]).reshape(128, 128))

    pa, pb = Portion("a"), Portion("b")
    state = s["state"]

    def z_step(step):
        up, down = 3 + (step - 1), 3 - (step - 1)
        if step < 4:
            pairs = [(up, up + 1, 15, pl.ds(0, 8)), (down, down - 1, 1, pl.ds(0, 8))]
        else:
            pairs = [(6, 7, 15, pl.ds(0, 4)), (0, 7, 1, pl.ds(4, 4))]
        return [copy(state.at[src, part], state.at[dst, part], dev(dz=dz)) for src, dst, dz, part in pairs]

    def where(j):
        return lax.rem(lax.rem(lax.div(j, 2), 8) - zl + 11, 8), lax.div(j, 16) * 2 + lax.rem(j, 2)

    def wcopy(c, part, where_to):
        return copy(wall.at[c, part], wall.at[c, part], where_to)

    all_z = pl.ds(0, 8)
    left_c, right_c = xs[3] * 2 + core, xs[1] * 2 + core
    far_c = xs[2] * 2 + core
    own_n = new_of(0, 0)

    attention(0)
    attention(1)
    fetches["tok"].wait()
    partial("a")
    pa.send_core()
    attention(2)
    pa.send_q1()
    attention(3)
    partial("b")
    pb.send_core()
    arrive(along_z)
    arrive(first)
    ring = z_step(1)
    pb.send_q1()
    along_x = [wcopy(me_c, all_z, dev(dx=1)), wcopy(me_c, all_z, dev(dx=3))]
    across = [wcopy(me_c, all_z, dev(dc=1))]
    arrive(ring)
    ring = z_step(2)
    pa.send_q2()
    arrive(ring)
    ring = z_step(3)
    pb.send_q2()
    pa.sum_q2()
    pb.sum_q2()

    z_out, z_in, z_all = s["z_out"], s["z_in"], s["z_all"]
    z_copies = []
    for r in sorted(range(1, 16), key=lambda r: -min(r, 16 - r)):
        z_copies.append(copy(z_out.at[:, lax.rem(zl + r, 8)], z_in.at[r - 1], dev(dz=r)))
    arrive(along_x)
    far = [wcopy(left_c, pl.ds(0, 4), dev(dx=1)), wcopy(right_c, pl.ds(4, 4), dev(dx=3))]
    across += [wcopy(left_c, all_z, dev(dc=1)), wcopy(right_c, all_z, dev(dc=1))]
    arrive(ring)
    ring = z_step(4)
    s["vacc"][...] = jnp.zeros((256, 256), F32)
    s["lacc"][...] = jnp.zeros((8, 256), F32)
    arrive(z_copies)
    t = s["z_sum"][:, zl]
    for r in range(15):
        t = t + f(z_in[r])
    z_all[:, zl] = t.astype(BF)
    gathered = [copy(z_all.at[:, zl], z_all.at[:, zl], dev(dz=o)) for o in (4, 13, 3, 14, 2, 15, 1)]

    arrive(ring)
    moved = []
    for idx, (dq, dc) in enumerate(GROUP):
        n = new_of(dq, dc)
        for i in range(2):
            slot, c = where(table_ref[2 * n + i])
            s["mv_pick"][idx, i] = state[slot, c]
        moved.append(copy(s["mv_pick"].at[idx], s["mv_in"].at[me_c], dev(dx=dq, dc=dc)))
    for i in range(2):
        slot, c = where(table_ref[2 * own_n + i])
        s["mv_in"][me_c, i] = state[slot, c]
    arrive(far)
    across.append(wcopy(far_c, all_z, dev(dc=1)))
    arrive(gathered)
    pa.gather_q2()
    pb.gather_q2()

    wnat = s["wnat"]
    arrive(across)

    def natural(i, _):
        slot, c = where(table_ref[i])
        base = pl.multiple_of(i * 64, 64)
        for piece in range(8):
            wnat[pl.ds(base + 16 * (piece // 2), 16), 128 * (piece % 2):128 * (piece % 2) + 128] = wall[c, slot, piece]
        return 0

    lax.fori_loop(0, 64, natural, 0, unroll=2)

    def project(i, _):
        k = pl.ds(pl.multiple_of(i * 512, 512), 512)
        s["vacc"][...] += jnp.dot(tok_ref[:, k], wnat[k, :], preferred_element_type=F32)
        return 0

    lax.fori_loop(0, 8, project, 0)
    for i in range(2):
        pair = s["vacc"][:, 128 * i:128 * i + 128]
        for odd in range(2):
            s["vals2"][2 * i + odd] = doubled(pair, odd).astype(BF)

    def loss_step(q, _):
        cot = cot_ref[:, pl.ds(pl.multiple_of(q * 128, 128), 128)]
        t = lax.dot_general(s["vals2"][lax.div(q, 4)], cot, (((1,), (1,)), ((), ())), preferred_element_type=F32)
        t = t * f(s["probs"][q])
        s["lacc"][...] += jnp.sum(t.reshape(64, 8, 256), axis=0)
        return 0

    pa.exchange()
    pb.exchange()
    lax.fori_loop(0, 16, loss_step, 0)
    loss_ref[...] = jnp.sum(s["lacc"][...], axis=0, keepdims=True)

    arrive(moved)
    for made in pending[:-14]:
        made.wait_send()
    grads = [pa.gradient(), pb.gradient()]
    for i in range(2):
        slot, src = where(table_ref[2 * own_n + i])
        for c in range(8):
            r0, l0 = 64 * i + 16 * (c // 2), 128 * (c % 2)
            weight = f(wall[src, slot, c])
            one = f(s["mv_in"][c, i, 0:16])
            two = f(s["mv_in"][c, i, 16:32])
            new = adam_step(weight, one, two, grads[c % 2][r0:r0 + 16])
            for ref, value in zip((wo_ref, mo_ref, vo_ref), new):
                ref[r0:r0 + 16, l0:l0 + 128] = value
    for made in pending[-14:]:
        made.wait_send()


def shards(
    tokens, queries, key_vectors, cotangent, positions, doc_ids, weight, moment_one, moment_two, old_ids, new_ids
):
    index = jnp.arange(64, dtype=jnp.int32)
    entry = jnp.arange(128, dtype=jnp.int32)
    table = jnp.sum(
        jnp.where(old_ids[None, :] == entry[:, None], index[None, :], 0)
        + jnp.where(index[None, :] + 64 == entry[:, None], new_ids[None, :], 0),
        axis=1,
    )
    lane = jnp.arange(256, dtype=jnp.int32)
    half = (lane % 32).astype(F32)
    frequency = rope_base ** (-(half * 2.0 / 64))
    angles = positions.astype(F32)[:, None] * frequency[None, :]
    signed = jnp.where((lane % 64) < 32, -jnp.sin(angles), jnp.sin(angles))
    trig = jnp.where(lane < 128, jnp.cos(angles), signed)

    vmem = pl.BlockSpec(memory_space=pltpu.VMEM)
    smem = pl.BlockSpec(memory_space=pltpu.SMEM)
    outs = pl.pallas_call(
        kernel,
        out_shape=[jax.ShapeDtypeStruct((128, 256), F32)] * 3 + [jax.ShapeDtypeStruct((1, 256), F32)],
        in_specs=[smem, vmem] + [pl.BlockSpec(memory_space=pl.ANY)] * 8,
        out_specs=[vmem] * 4,
        scratch_shapes=list(PLAN.values()),
        compiler_params=pltpu.CompilerParams(
            collective_id=0, has_side_effects=True, vmem_limit_bytes=54144 * 1024
        ),
        cost_estimate=pl.CostEstimate(flops=2_200_000_000, bytes_accessed=6_000_000, transcendentals=2_200_000),
    )(
        table, trig, weight, moment_one, moment_two, key_vectors, doc_ids.reshape(1, 256), queries, cotangent, tokens
    )
    return (outs[0], outs[1], outs[2], outs[3].reshape(256))


def solution(mesh):
    in_specs = (
        P(("rep", "fsdp"), None),
        P(("rep", "fsdp"), None),
        P(("rep", "fsdp"), None),
        P(("rep", "fsdp"), None),
        P(("rep", "fsdp")),
        P(("rep", "fsdp")),
        P("fsdp", None),
        P("fsdp", None),
        P("fsdp", None),
        P(),
        P(),
    )
    out_specs = (P("fsdp", None), P("fsdp", None), P("fsdp", None), P(("rep", "fsdp")))
    return jax.shard_map(shards, mesh=mesh, in_specs=in_specs, out_specs=out_specs, check_vma=False)
```

time: 98.5 us -> 75.2 us (0.76)
  the two profiles are of different devices: /device:TPU:32 before, /device:TPU:1 now
where the time goes in v2:
time: 75.2 us; the launch traced here: 74.9 us
  Pallas kernels  65.1 us (87%)
  local copies, waits for them, and re-layouts  6.63 us (9%)
  other arithmetic  2.5 us (3%)
    pallas_call x1, Pallas kernels, shards(): pl.pallas_call(kernel, out_shape=[jax.ShapeDtypeStruct((128, 256), F32)]...  65.1 us
    unnamed x14, local copies, waits for them, and re-layouts  6.63 us

profile of v2, /device:TPU:1, one launch (start us, length us, event | category | flops | bytes accessed | tf_op | source)
XLA Modules:
  0.0 74.9 jit_solution(6684413034615884027)
XLA Ops:
  0.6 0.8 %add_reduce_fusion.table_ref = s32[128]{0:T(128)S(1)} fusion(s32[64]{0:T(128)} %param.21, s32[64]{0:T(128)S(1)} %iota_add_fusion, s32[64]{0:T(128)} %param.20), kind=kLoop, calls=%fused_computation.4 | loop fusion | flops 49024 | bytes 1280 | tf_op jit(solution)/shard_map/reduce_sum | solution.py:472
  1.4 0.7 convert_element_type.10
  2.1 1.0 %fusion.trig_ref = f32[256,256]{1,0:T(8,128)S(1)} fusion(f32[256]{0:T(256)S(1)} %fusion.4, f32[256]{0:T(256)S(1)} %convert_element_type.10, pred[256]{0:T(512)(128)(4,1)S(1)} %get-tuple-element.12, pred[256]{0:T(512)(128)(4,1)S(1)} %get-tuple-element.13), kind=kLoop, calls=%fused_computation.3 | loop fusion | flops 262144 | bytes 264704 | tf_op jit(solution)/shard_map/jit(_where)/select_n | solution.py:482
  3.1 0.0 copy-start
  3.2 0.9 %copy-done = bf16[256,256]{1,0:T(8,128)(2,1)S(1)} copy-done((bf16[256,256]{1,0:T(8,128)(2,1)S(1)}, bf16[256,256]{1,0:T(8,128)(2,1)}, u32[]{:S(2)}) %copy-start) | copy-done | bytes 131096
  4.1 0.0 copy-start.1
  4.1 0.8 %copy-done.1 = f32[64,256]{1,0:T(8,128)S(1)} copy-done((f32[64,256]{1,0:T(8,128)S(1)}, f32[64,256]{1,0:T(8,128)}, u32[]{:S(2)}) %copy-start.1) | copy-done | bytes 65560
  4.9 0.0 copy-start.2
  4.9 0.8 %copy-done.2 = f32[64,256]{1,0:T(8,128)S(1)} copy-done((f32[64,256]{1,0:T(8,128)S(1)}, f32[64,256]{1,0:T(8,128)}, u32[]{:S(2)}) %copy-start.2) | copy-done | bytes 65560
  5.7 0.0 copy-start.3
  5.7 0.8 %copy-done.3 = f32[64,256]{1,0:T(8,128)S(1)} copy-done((f32[64,256]{1,0:T(8,128)S(1)}, f32[64,256]{1,0:T(8,128)}, u32[]{:S(2)}) %copy-start.3) | copy-done | bytes 65560
  6.6 0.0 copy-start.4
  6.6 0.7 copy-done.4
  7.3 65.1 %shard_map.138 = (f32[128,256]{1,0:T(8,128)S(1)}, f32[128,256]{1,0:T(8,128)S(1)}, f32[128,256]{1,0:T(8,128)S(1)}, f32[1,256]{1,0:T(1,128)S(1)}) custom-call(s32[128]{0:T(128)S(1)} %add_reduce_fusion.table_ref, f32[256,256]{1,0:T(8,128)S(1)} %fusion.trig_ref, f32[64,256]{1,0:T(8,128)S(1)} %copy-done.1, f32[64,256]{1,0:T(8,128)S(1)} %copy-done.2, ...), custom_call_target="tpu_custom_call" | custom-call | flops 2200000000 | bytes 6000000 | tf_op jit(solution)/shard_map/pallas_call | solution.py:486
  72.4 0.7 copy.19
  73.0 0.7 copy.20
  73.7 0.7 copy.21
  74.4 0.6 copy.22
  (3 shorter events, 0.0 us)
Async XLA Ops:
  3.1 0.9 %copy-start = (bf16[256,256]{1,0:T(8,128)(2,1)S(1)}, bf16[256,256]{1,0:T(8,128)(2,1)}, u32[]{:S(2)}) copy-start(bf16[256,256]{1,0:T(8,128)(2,1)} %k_hbm.1) | copy-start | bytes 393220
  4.1 0.8 %copy-start.1 = (f32[64,256]{1,0:T(8,128)S(1)}, f32[64,256]{1,0:T(8,128)}, u32[]{:S(2)}) copy-start(f32[64,256]{1,0:T(8,128)} %w_hbm.1) | copy-start | bytes 196612
  4.9 0.8 %copy-start.2 = (f32[64,256]{1,0:T(8,128)S(1)}, f32[64,256]{1,0:T(8,128)}, u32[]{:S(2)}) copy-start(f32[64,256]{1,0:T(8,128)} %m_hbm.1) | copy-start | bytes 196612
  5.7 0.8 %copy-start.3 = (f32[64,256]{1,0:T(8,128)S(1)}, f32[64,256]{1,0:T(8,128)}, u32[]{:S(2)}) copy-start(f32[64,256]{1,0:T(8,128)} %v_hbm.1) | copy-start | bytes 196612
  6.6 0.7 copy-start.4

commit v3 on v2

--- a/solution.py
+++ b/solution.py
@@ -70,19 +70,14 @@
         z_all=pltpu.VMEM((2, 8, 16, 128), BF),
         tok=pltpu.VMEM((TOK, 4096), BF),
         q=pltpu.VMEM((TOK, 2048), BF),
-        k=pltpu.VMEM((TOK, 256), BF),
         cot=pltpu.VMEM((TOK, 2048), BF),
-        doc=pltpu.VMEM((1, TOK), jnp.int32),
-        w=pltpu.VMEM((64, 256), F32),
-        m=pltpu.VMEM((64, 256), F32),
-        v=pltpu.VMEM((64, 256), F32),
     )
     for name in "ab":
         for key, value in portion_scratch().items():
             plan[name + "_" + key] = value
     plan["send"] = pltpu.SemaphoreType.DMA((112,))
     plan["recv"] = pltpu.SemaphoreType.DMA((112,))
-    plan["local"] = pltpu.SemaphoreType.DMA((8,))
+    plan["local"] = pltpu.SemaphoreType.DMA((3,))
     return plan
 
 
@@ -99,18 +94,14 @@
 
 
 def kernel(
-    table_ref, trig_ref, w_hbm, m_hbm, v_hbm, k_hbm, doc_hbm, q_hbm, cot_hbm, tok_hbm,
-    wo_ref, mo_ref, vo_ref, loss_ref, *scratch
+    table_ref, trig_ref, small_ref, k_ref, doc_ref, q_hbm, cot_hbm, tok_hbm,
+    wo_ref, mo_ref, vo_ref, go_ref, loss_ref, *scratch
 ):
     s = dict(zip(PLAN, scratch))
     send, recv = s["send"], s["recv"]
-    w_ref, m_ref, v_ref, k_ref, doc_ref, q_ref, cot_ref, tok_ref = (
-        s[name] for name in ("w", "m", "v", "k", "doc", "q", "cot", "tok")
-    )
+    q_ref, cot_ref, tok_ref = s["q"], s["cot"], s["tok"]
     fetches = {}
-    for idx, (name, src) in enumerate(
-        zip(("w", "m", "v", "k", "doc", "q", "cot", "tok"), (w_hbm, m_hbm, v_hbm, k_hbm, doc_hbm, q_hbm, cot_hbm, tok_hbm))
-    ):
+    for idx, (name, src) in enumerate(zip(("q", "cot", "tok"), (q_hbm, cot_hbm, tok_hbm))):
         fetches[name] = pltpu.make_async_copy(src, s[name], s["local"].at[idx])
         fetches[name].start()
     rep = lax.axis_index("rep")
@@ -166,21 +157,18 @@
         swapped = jnp.where(low_half, pltpu.roll(pair, 96, 1), pltpu.roll(pair, 32, 1))
         return pair * trig_ref[:, 0:128] + swapped * trig_ref[:, 128:256]
 
-    for name in ("w", "m", "v"):
-        fetches[name].wait()
     for c in range(8):
-        rows, cols = pl.ds(16 * (c // 2), 16), pl.ds(128 * (c % 2), 128)
-        s["wall"][me_c, 3, c] = w_ref[rows, cols].astype(BF)
-        for part, ref in enumerate((m_ref, v_ref)):
-            s["state_out"][c, 16 * part:16 * part + 16] = ref[rows, cols].astype(BF)
+        r0, l0 = 16 * (c // 2), 128 * (c % 2)
+        s["wall"][me_c, 3, c] = small_ref[r0:r0 + 16, l0:l0 + 128].astype(BF)
+        for part in range(2):
+            moment = small_ref[64 + 64 * part + r0:80 + 64 * part + r0, l0:l0 + 128]
+            s["state_out"][c, 16 * part:16 * part + 16] = moment.astype(BF)
     s["state"][3, me_c] = s["state_out"][me_c]
 
-    fetches["k"].wait()
     for i in range(2):
         turned = rotated(k_ref[:, 128 * i:128 * i + 128].astype(F32))
         for odd in range(2):
             s["keys2"][2 * i + odd] = doubled(turned, odd).astype(BF)
-    fetches["doc"].wait()
     docs = doc_ref[...].astype(F32)
     columns = jnp.transpose(jnp.broadcast_to(docs, (128, TOK)))
     own_row = lax.broadcasted_iota(jnp.int32, (TOK, 128), 0)
@@ -188,14 +176,6 @@
         allowed = (own_row <= lane128 + 128 * half) & (columns == docs[:, 128 * half:128 * half + 128])
         s["bias"][:, 128 * half:128 * half + 128] = jnp.where(allowed, 0.0, -1e30)
 
-    pl.semaphore_wait(barrier, len(partners))
-    wall = s["wall"]
-    own_w = wall.at[me_c, 3]
-    along_z = [copy(own_w, wall.at[me_c, 3 - o], dev(dz=o)) for o in (-4, 3, -3, 2, -2, 1, -1)]
-    first = []
-    for dq, dc in GROUP:
-        to_c = xs[dq] * 2 + cores[dc]
-        first.append(copy(s["state_out"].at[to_c], s["state"].at[3, me_c], dev(dx=dq, dc=dc)))
     fetches["q"].wait()
     fetches["cot"].wait()
     factor = 0.125 * math.log2(math.e)
@@ -250,7 +230,7 @@
             body(pl.ds(i * step, step))
             return 0
 
-        lax.fori_loop(0, n // step, run, 0)
+        lax.fori_loop(0, n // step, run, 0, unroll=2)
 
     class Portion:
         def __init__(self, name):
@@ -353,6 +333,14 @@
 
     attention(0)
     attention(1)
+    pl.semaphore_wait(barrier, len(partners))
+    wall = s["wall"]
+    own_w = wall.at[me_c, 3]
+    along_z = [copy(own_w, wall.at[me_c, 3 - o], dev(dz=o)) for o in (-4, 3, -3, 2, -2, 1, -1)]
+    first = []
+    for dq, dc in GROUP:
+        to_c = xs[dq] * 2 + cores[dc]
+        first.append(copy(s["state_out"].at[to_c], s["state"].at[3, me_c], dev(dx=dq, dc=dc)))
     fetches["tok"].wait()
     partial("a")
     pa.send_core()
@@ -447,19 +435,17 @@
     loss_ref[...] = jnp.sum(s["lacc"][...], axis=0, keepdims=True)
 
     arrive(moved)
-    for made in pending[:-14]:
-        made.wait_send()
-    grads = [pa.gradient(), pb.gradient()]
     for i in range(2):
         slot, src = where(table_ref[2 * own_n + i])
         for c in range(8):
             r0, l0 = 64 * i + 16 * (c // 2), 128 * (c % 2)
-            weight = f(wall[src, slot, c])
-            one = f(s["mv_in"][c, i, 0:16])
-            two = f(s["mv_in"][c, i, 16:32])
-            new = adam_step(weight, one, two, grads[c % 2][r0:r0 + 16])
-            for ref, value in zip((wo_ref, mo_ref, vo_ref), new):
-                ref[r0:r0 + 16, l0:l0 + 128] = value
+            wo_ref[r0:r0 + 16, l0:l0 + 128] = f(wall[src, slot, c])
+            mo_ref[r0:r0 + 16, l0:l0 + 128] = f(s["mv_in"][c, i, 0:16])
+            vo_ref[r0:r0 + 16, l0:l0 + 128] = f(s["mv_in"][c, i, 16:32])
+    for made in pending[:-14]:
+        made.wait_send()
+    go_ref[:, 0:128] = pa.gradient()
+    go_ref[:, 128:256] = pb.gradient()
     for made in pending[-14:]:
         made.wait_send()
 
@@ -480,23 +466,22 @@
     angles = positions.astype(F32)[:, None] * frequency[None, :]
     signed = jnp.where((lane % 64) < 32, -jnp.sin(angles), jnp.sin(angles))
     trig = jnp.where(lane < 128, jnp.cos(angles), signed)
+    small = jnp.concatenate([weight, moment_one, moment_two], axis=0)
 
     vmem = pl.BlockSpec(memory_space=pltpu.VMEM)
     smem = pl.BlockSpec(memory_space=pltpu.SMEM)
     outs = pl.pallas_call(
         kernel,
-        out_shape=[jax.ShapeDtypeStruct((128, 256), F32)] * 3 + [jax.ShapeDtypeStruct((1, 256), F32)],
-        in_specs=[smem, vmem] + [pl.BlockSpec(memory_space=pl.ANY)] * 8,
-        out_specs=[vmem] * 4,
+        out_shape=[jax.ShapeDtypeStruct((128, 256), F32)] * 4 + [jax.ShapeDtypeStruct((1, 256), F32)],
+        in_specs=[smem] + [vmem] * 4 + [pl.BlockSpec(memory_space=pl.ANY)] * 3,
+        out_specs=[vmem] * 5,
         scratch_shapes=list(PLAN.values()),
         compiler_params=pltpu.CompilerParams(
-            collective_id=0, has_side_effects=True, vmem_limit_bytes=54144 * 1024
+            collective_id=0, has_side_effects=True, vmem_limit_bytes=53760 * 1024
         ),
         cost_estimate=pl.CostEstimate(flops=2_200_000_000, bytes_accessed=6_000_000, transcendentals=2_200_000),
-    )(
-        table, trig, weight, moment_one, moment_two, key_vectors, doc_ids.reshape(1, 256), queries, cotangent, tokens
-    )
-    return (outs[0], outs[1], outs[2], outs[3].reshape(256))
+    )(table, trig, small, key_vectors, doc_ids.reshape(1, 256), queries, cotangent, tokens)
+    return adam_step(*outs[:4]) + (outs[4].reshape(256),)
 
 
 def solution(mesh):

time: 75.2 us -> 68.8 us (0.915)
  local copies, waits for them, and re-layouts: 6.63 us -> 2.14 us
  Pallas kernels: 65.1 us -> 61.5 us
  other arithmetic: 2.5 us -> 4.22 us
    unnamed x14 -> x5, local copies, waits for them, and re-layouts: 6.63 us -> 2.14 us
    pallas_call x1, Pallas kernels: 65.1 us -> 61.5 us  [shards(): pl.pallas_call(kernel, out_shape=[jax.ShapeDtypeStruct((128, 256), F32)]...]
    concatenate x0 -> x1, other arithmetic: none -> 0.92 us  [shards(): small = jnp.concatenate([weight, moment_one, moment_two], axis=0)]
    sub x0 -> x1, other arithmetic: none -> 0.8 us  [adam_step(): weight_new = weight - learn_rate * (update + decay_rate * weight)]
where the time goes in v3:
time: 68.8 us; the launch traced here: 68.6 us
  Pallas kernels  61.5 us (89%)
  other arithmetic  4.22 us (6%)
  local copies, waits for them, and re-layouts  2.14 us (3%)
    pallas_call x1, Pallas kernels, shards(): pl.pallas_call(kernel, out_shape=[jax.ShapeDtypeStruct((128, 256), F32)]...  61.5 us
    unnamed x5, local copies, waits for them, and re-layouts  2.14 us

profile of v3, /device:TPU:1, one launch (start us, length us, event | category | flops | bytes accessed | tf_op | source)
XLA Modules:
  0.0 68.6 jit_solution(13254526722793493911)
XLA Ops:
  0.6 0.8 %add_reduce_fusion.table_ref = s32[128]{0:T(128)S(1)} fusion(s32[64]{0:T(128)} %param.21, s32[64]{0:T(128)S(1)} %iota_add_fusion, s32[64]{0:T(128)} %param.20), kind=kLoop, calls=%fused_computation.9 | loop fusion | flops 49024 | bytes 1280 | tf_op jit(solution)/shard_map/reduce_sum | solution.py:458
  1.4 0.7 %convert_element_type.10 = f32[256]{0:T(256)S(1)} convert(s32[256]{0:T(256)} %param.15) | non-fusion elementwise | flops 256 | bytes 2048 | tf_op jit(solution)/shard_map/convert_element_type | solution.py:466
  2.1 0.9 %pad_maximum_fusion.small_ref = f32[192,256]{1,0:T(8,128)S(1)} fusion(f32[64,256]{1,0:T(8,128)} %param.19, f32[64,256]{1,0:T(8,128)} %param.18, f32[64,256]{1,0:T(8,128)} %param.17), kind=kLoop, calls=%fused_computation.4 | loop fusion | flops 98304 | bytes 393216 | tf_op jit(solution)/shard_map/concatenate | solution.py:469
  3.0 1.0 %fusion.trig_ref = f32[256,256]{1,0:T(8,128)S(1)} fusion(f32[256]{0:T(256)S(1)} %fusion.5, f32[256]{0:T(256)S(1)} %convert_element_type.10, pred[256]{0:T(512)(128)(4,1)S(1)} %get-tuple-element.17, pred[256]{0:T(512)(128)(4,1)S(1)} %get-tuple-element.18), kind=kLoop, calls=%fused_computation.3 | loop fusion | flops 262144 | bytes 264704 | tf_op jit(solution)/shard_map/jit(_where)/select_n | solution.py:468
  4.1 0.0 copy-start
  4.1 0.9 %copy-done = bf16[256,256]{1,0:T(8,128)(2,1)S(1)} copy-done((bf16[256,256]{1,0:T(8,128)(2,1)S(1)}, bf16[256,256]{1,0:T(8,128)(2,1)}, u32[]{:S(2)}) %copy-start) | copy-done | bytes 131096
  5.0 0.0 copy-start.1
  5.0 0.7 copy-done.1
  5.7 61.5 %shard_map.138 = (f32[128,256]{1,0:T(8,128)S(1)}, f32[128,256]{1,0:T(8,128)S(1)}, f32[128,256]{1,0:T(8,128)S(1)}, f32[128,256]{1,0:T(8,128)S(1)}, f32[1,256]{1,0:T(1,128)S(1)}) custom-call(s32[128]{0:T(128)S(1)} %add_reduce_fusion.table_ref, f32[256,256]{1,0:T(8,128)S(1)} %fusion.trig_ref, f32[192,256]{1,0:T(8,128)S(1)} %pad_maximum_fusion.small_ref, ...), custom_call_target="tpu_custom_call" | custom-call | flops 2200000000 | bytes 6000000 | tf_op jit(solution)/shard_map/pallas_call | solution.py:473
  67.2 0.8 %multiply_subtract_fusion = (f32[128,256]{1,0:T(8,128)}, f32[128,256]{1,0:T(8,128)}, f32[128,256]{1,0:T(8,128)}) fusion(f32[128,256]{1,0:T(8,128)S(1)} %get-tuple-element.9, f32[128,256]{1,0:T(8,128)S(1)} %get-tuple-element.11, f32[128,256]{1,0:T(8,128)S(1)} %get-tuple-element.10, f32[128,256]{1,0:T(8,128)S(1)} %get-tuple-element.12), kind=kLoop, calls=%fused_computation.7 | loop fusion | flops 491520 | bytes 917504 | tf_op jit(solution)/shard_map/sub | solution.py:33
  68.0 0.6 copy.16
  (3 shorter events, 0.0 us)
Async XLA Ops:
  4.1 0.9 %copy-start = (bf16[256,256]{1,0:T(8,128)(2,1)S(1)}, bf16[256,256]{1,0:T(8,128)(2,1)}, u32[]{:S(2)}) copy-start(bf16[256,256]{1,0:T(8,128)(2,1)} %k_ref.1) | copy-start | bytes 393220
  5.0 0.7 copy-start.1
